TPU v7x, 32 devices: a whole 2x2x4 slice. The times are simulated.
32 devices in a mesh: seg: 8 (over z, x), grp: 4 (over y, core).
Axes of the slice: x: 2, y: 2, z: 4, core: 2. Of those that a mesh axis runs over, the one named last changes fastest.
Arguments:
- snapshots: float32 [49152, 512], P(('seg', 'grp')), as said below
- upstream: int32 [49152], P(('seg', 'grp')), may hold values from -1 to 49150, as said below
- velocity: float32 [49152], P(('seg', 'grp')), may hold values from 0.5 to 4
Outputs:
- reduced_operator: float32 [512, 512], replicated
- triangle: float32 [512, 512], replicated
Inputs may be any that keep to these rules, and one draw needn't show every extreme that they name: Segment g = p * 1536 + l lies in partition p. For l >= 512 its upstream is a segment of the same partition with a smaller index, and for l = 1535 it is g - 1. For l < 512 its upstream lies in the last 512 segments of partition p - 1, and the first segment of each partition p >= 1 takes exactly segment p * 1536 - 512; in partition 0 these segments have upstream -1, and no other segment has. `snapshots`: Real-valued fields of full rank.
All inputs are finite; a program needn't handle non-finite values.
Results may differ from a plain program's by a relative error of at most 0.0003.
Values sent between devices are 32-bit elements; how exact they have to be, the bound alone decides.
A program may use at most 128 MiB of HBM per device.

v0:
```python
import jax
import jax.numpy as jnp
from jax import lax
from jax.experimental import pallas as pl
from jax.experimental.pallas import tpu as pltpu
from jax.sharding import PartitionSpec as P

EDGE = 512
NB = 64
GROUP = 4
AXES = ("seg", "grp")


def dot32(a, b, dims):
    return lax.dot_general(
        a,
        b,
        (dims, ((), ())),
        precision=lax.Precision.HIGHEST,
        preferred_element_type=jnp.float32,
    )


def eliminate(block):
    rows = lax.broadcasted_iota(jnp.int32, (NB, 2 * NB), 0)
    lanes = lax.broadcasted_iota(jnp.int32, (NB, 2 * NB), 1)
    unit = (rows + NB == lanes).astype(jnp.float32)
    work = jnp.concatenate([block, unit[:, NB:]], 1)
    for k in range(0, NB, GROUP):
        cols = [
            jnp.broadcast_to(work[:, k + i : k + i + 1], (NB, 2 * NB))
            for i in range(GROUP)
        ]
        lines = [work[k + i : k + i + 1, :] for i in range(GROUP)]
        piv = [[cols[j][k + i : k + i + 1, :] for j in range(GROUP)] for i in range(GROUP)]
        for i in range(GROUP):
            inv = 1.0 / piv[i][i]
            scaled = lines[i] * inv
            below = jnp.where(rows > k + i, cols[i], 0.0)
            work = work - below * scaled
            for j in range(i + 1, GROUP):
                f = piv[j][i] * inv
                lines[j] = lines[j] - f * lines[i]
                g = piv[i][j] * inv
                cols[j] = cols[j] - below * g
                for m in range(i + 1, GROUP):
                    piv[j][m] = piv[j][m] - f * piv[i][m]
    diag = jnp.sum(jnp.where(rows == lanes, work, 0.0), axis=1, keepdims=True)
    work = work * lax.rsqrt(diag)
    keep = (lanes >= rows) & ((lanes < NB) | (lanes <= rows + NB))
    return jnp.where(keep, work, 0.0)


def factor_kernel(gram_ref, upper_ref, inverse_ref, a_ref):
    order = gram_ref.shape[0]
    a_ref[...] = gram_ref[...]
    upper_ref[...] = jnp.zeros_like(upper_ref)
    r = lax.broadcasted_iota(jnp.int32, (order, order), 0)
    c = lax.broadcasted_iota(jnp.int32, (order, order), 1)
    inverse_ref[...] = (r == c).astype(jnp.float32)
    for lo in range(0, order, NB):
        hi = lo + NB
        done = eliminate(a_ref[lo:hi, lo:hi])
        inv = done[:, NB:]
        upper_ref[lo:hi, lo:hi] = done[:, :NB]
        new = dot32(inv, inverse_ref[lo:hi, :], ((1,), (0,)))
        inverse_ref[lo:hi, :] = new
        if hi < order:
            line = dot32(inv, a_ref[lo:hi, hi:], ((1,), (0,)))
            upper_ref[lo:hi, hi:] = line
            a_ref[hi:, hi:] = a_ref[hi:, hi:] - dot32(line, line, ((0,), (0,)))
            inverse_ref[hi:, :] = inverse_ref[hi:, :] - dot32(line, new, ((0,), (0,)))


def factor(gram):
    order = gram.shape[0]
    shape = jax.ShapeDtypeStruct((order, order), jnp.float32)
    return pl.pallas_call(
        factor_kernel,
        out_shape=(shape, shape),
        in_specs=[pl.BlockSpec(memory_space=pltpu.VMEM)],
        out_specs=(pl.BlockSpec(memory_space=pltpu.VMEM),) * 2,
        scratch_shapes=[pltpu.VMEM((order, order), jnp.float32)],
        compiler_params=pltpu.CompilerParams(vmem_limit_bytes=32 * 1024 * 1024),
        cost_estimate=pl.CostEstimate(
            flops=12 * order**3, bytes_accessed=12 * order**2, transcendentals=0
        ),
    )(gram)


def from_behind(block):
    count = lax.axis_size(AXES)
    route = [(i - 1, i) for i in range(1, count)]
    return lax.ppermute(block, AXES, route)


def shards(snapshots, upstream, velocity):
    high = lax.Precision.HIGH
    rows_here = snapshots.shape[0]
    count = rows_here * lax.axis_size(AXES)
    first_row = lax.axis_index(AXES) * rows_here
    arrived = from_behind(snapshots[rows_here - EDGE :])
    local_gram = jnp.dot(
        snapshots.T, snapshots, precision=high, preferred_element_type=jnp.float32
    )
    gram = lax.psum(local_gram, AXES) / count
    extended = jnp.concatenate([arrived, snapshots], 0)
    position = upstream - (first_row - EDGE)
    image = velocity[:, None] * (jnp.take(extended, position, axis=0) - snapshots)
    local_term = jnp.dot(
        snapshots.T, image, precision=high, preferred_element_type=jnp.float32
    )
    term = lax.psum(local_term, AXES) / count
    upper, inverse = factor(gram)
    operator = dot32(dot32(inverse, term, ((1,), (0,))), inverse, ((1,), (1,)))
    return (operator, upper)


def solution(mesh):
    return jax.shard_map(
        shards,
        mesh=mesh,
        in_specs=(P(AXES, None), P(AXES), P(AXES)),
        out_specs=(P(), P()),
        check_vma=False,
    )
```

profile of v0, /device:TPU:0, one launch (start us, length us, event | category | flops | bytes accessed | tf_op | source)
XLA Modules:
  0.0 219.8 jit_solution(8409199250994386627)
XLA Ops:
  7.2 0.0 all-reduce.3.cloned.1.call-start
  7.2 2.3 %slice.3 = f32[512,512]{1,0:T(8,128)} slice(f32[1536,512]{1,0:T(8,128)} %param.3), slice={[1024:1536], [0:512]} | slice | bytes 2097152 | tf_op jit(solution)/shard_map/slice | solution.py:102
  9.5 3.3 %collective-permute-start = (f32[512,512]{1,0:T(8,128)}, f32[512,512]{1,0:T(8,128)}, u32[]{:S(2)}, u32[]{:S(2)}) collective-permute-start(f32[512,512]{1,0:T(8,128)} %slice.3), channel_id=1, source_target_pairs={{0,1},{1,2},{2,3},{3,4},{4,5},{5,6},{6,7},{7,8},{8,9},{9,10},{10,1... | collective-permute-start | bytes 3145736 | tf_op jit(solution)/shard_map/ppermute | solution.py:94
  12.8 0.7 compare_and_fusion
  13.5 0.0 copy-start
  13.5 6.6 %fusion.15 = f32[512,512]{1,0:T(8,128)} fusion(f32[1536,512]{1,0:T(8,128)} %param.3), kind=kOutput, calls=%fused_computation.19 | convolution fusion | flops 2415919104 | bytes 4194304 | tf_op jit(solution)/shard_map/dot_general | solution.py:103
  20.1 0.0 collective-permute-done
  20.1 0.0 copy-done
  20.1 3.6 %pad_maximum_fusion = f32[2048,512]{1,0:T(8,128)} fusion(f32[1536,512]{1,0:T(8,128)S(1)} %copy-done, f32[512,512]{1,0:T(8,128)} %collective-permute-done), kind=kLoop, calls=%fused_computation.1 | loop fusion | flops 1048576 | bytes 8388608 | tf_op jit(solution)/shard_map/concatenate | solution.py:107
  23.7 0.0 copy-start.2
  23.7 7.9 %gather_fusion = f32[1536,512]{1,0:T(8,128)} fusion(f32[2048,512]{1,0:T(8,128)} %pad_maximum_fusion, s32[2048]{0:T(1024)S(1)} %pad_clamp_fusion), kind=kCustom, calls=%fused_computation | custom fusion | bytes 6297600 | tf_op jit(solution)/shard_map/jit(_take)/gather | solution.py:109
  31.7 0.0 copy-done.2
  31.7 6.3 %fusion.7 = f32[512,512]{1,0:T(8,128)} fusion(f32[1536,512]{1,0:T(8,128)S(1)} %copy-done, f32[1536,512]{1,0:T(8,128)} %gather_fusion, f32[1536]{0:T(1024)S(1)} %copy-done.2, pred[1536]{0:T(1024)(128)(4,1)S(1)} %get-tuple-element.8), kind=kOutput, calls=%fused_computation.9 | convolution fusion | flops 2418278400 | bytes 7347712 | tf_op jit(solution)/shard_map/dot_general | solution.py:110
  38.0 0.0 all-reduce.3.cloned.1.call-update
  38.0 142.6 %all-reduce.3.cloned.1.call-done = (f32[512,512]{1,0:T(8,128)}, f32[512,512]{1,0:T(8,128)}) async-done(((f32[512,512]{1,0:T(8,128)}, f32[512,512]{1,0:T(8,128)}), (f32[512,512]{1,0:T(8,128)}, f32[512,512]{1,0:T(8,128)})) %all-reduce.3.cloned.1.call-update) | async-done | bytes 2097168 | tf_op jit(solution)/shard_map/psum | solution.py:106
  180.6 1.3 broadcast_multiply_fusion.gram_ref
  181.9 0.0 copy-start.1
  181.9 26.3 %shard_map.50 = (f32[512,512]{1,0:T(8,128)}, f32[512,512]{1,0:T(8,128)S(1)}) custom-call(f32[512,512]{1,0:T(8,128)S(1)} %broadcast_multiply_fusion.gram_ref), custom_call_target="tpu_custom_call" | custom-call | flops 1610612736 | bytes 3145728 | tf_op jit(solution)/shard_map/pallas_call | solution.py:78
  208.3 0.0 copy-done.1
  208.3 1.9 fusion.10
  210.1 2.8 %fusion.16 = f32[512,512]{1,0:T(8,128)} fusion(f32[512,512]{1,0:T(8,128)S(1)} %fusion.10, f32[512,512]{1,0:T(8,128)S(1)} %get-tuple-element.4), kind=kOutput, calls=%fused_computation.20 | convolution fusion | flops 1610612736 | bytes 3145728 | tf_op jit(solution)/shard_map/dot_general | solution.py:15
  (1 shorter events, 0.0 us)
Async XLA Ops:
  7.2 173.4 %all-reduce.3.cloned.1.call-start = ((), (), s32[]{:S(2)}) async-start(), calls=%async_computation | async-start | bytes 4194304 | tf_op jit(solution)/shard_map/psum | solution.py:106
  9.5 10.6 %collective-permute-start = (f32[512,512]{1,0:T(8,128)}, f32[512,512]{1,0:T(8,128)}, u32[]{:S(2)}, u32[]{:S(2)}) collective-permute-start(f32[512,512]{1,0:T(8,128)} %slice.3), channel_id=1, source_target_pairs={{0,1},{1,2},{2,3},{3,4},{4,5},{5,6},{6,7},{7,8},{8,9},{9,10},{10,1... | collective-permute-start | bytes 3145736 | tf_op jit(solution)/shard_map/ppermute | solution.py:94
  13.5 6.6 %copy-start = (f32[1536,512]{1,0:T(8,128)S(1)}, f32[1536,512]{1,0:T(8,128)}, u32[]{:S(2)}) copy-start(f32[1536,512]{1,0:T(8,128)} %param.3) | copy-start | bytes 9437188
  23.7 7.9 %copy-start.2 = (f32[1536]{0:T(1024)S(1)}, f32[1536]{0:T(1024)}, u32[]{:S(2)}) copy-start(f32[1536]{0:T(1024)} %param.5) | copy-start | bytes 18436
  181.9 26.3 %copy-start.1 = (f32[512,512]{1,0:T(8,128)S(1)}, f32[512,512]{1,0:T(8,128)}, u32[]{:S(2)}) copy-start(f32[512,512]{1,0:T(8,128)} %get-tuple-element.7) | copy-start | bytes 3145732
Sparse Core Ops, SparseCore 0:
  38.1 142.4 all-reduce.2
where the time goes:
time: 220 us
  waiting for transfers between devices  143 us (65%)
  Pallas kernels  26.3 us (12%)
  matrix products  17.6 us (8%)
  between operations  14.1 us (6%)
  local copies, waits for them, and re-layouts  10.2 us (5%)
  other arithmetic  5.65 us (3%)
  starting transfers between devices  3.35 us (2%)
    psum x1, waiting for transfers between devices, shards(): gram = lax.psum(local_gram, AXES) / count  143 us
    pallas_call x1, Pallas kernels, factor(): pl.pallas_call(factor_kernel, out_shape=(shape, shape), in_specs=[pl.Bloc...  26.3 us
    gather x1, local copies, waits for them, and re-layouts, shards(): jnp.take(extended, position, axis=0) - snapshots  7.94 us
    dot_general x1, matrix products, shards(): jnp.dot(snapshots.T, snapshots, precision=high, preferred_element_type=jn...  6.59 us
    dot_general x1, matrix products, shards(): jnp.dot(snapshots.T, image, precision=high, preferred_element_type=jnp.fl...  6.3 us
    dot_general x2, matrix products, dot32(): lax.dot_general(a, b, (dims, ((), ())), precision=lax.Precision.HIGHEST,...  4.7 us
  transfers between devices with their start and end apart: 2, of which 1 were waited for; matrix products, arithmetic and copies ran while one was open for 3% of the time, Pallas kernels for 0%

commit v1 on v0

--- a/solution.py
+++ b/solution.py
@@ -1,3 +1,5 @@
+import functools
+
 import jax
 import jax.numpy as jnp
 from jax import lax
@@ -88,6 +90,180 @@
     )(gram)
 
 
+TILE = 128
+
+
+def level_plan(rows, levels):
+    sizes = []
+    size = rows
+    for _ in range(levels):
+        if size % 16 == 0:
+            size //= 2
+            sizes.append((size, True))
+        else:
+            sizes.append((size, False))
+    return sizes
+
+
+def sum_kernel(
+    plans, orders, starts, landing, scale, width,
+    gram_ref, term_ref, gram_out, term_out,
+    part, inbox, full, send_sem, recv_sem,
+):
+    minor = lax.axis_size("grp")
+    me = lax.axis_index("seg") * minor + lax.axis_index("grp")
+    levels = len(orders[0])
+
+    def bit_of(b):
+        return (me // (1 << b)) % 2
+
+    def device(b):
+        other = me + (1 - 2 * bit_of(b)) * (1 << b)
+        return (other // minor, other % minor)
+
+    barrier = pltpu.get_barrier_semaphore()
+    for b in range(levels):
+        pl.semaphore_signal(
+            barrier, inc=1, device_id=device(b), device_id_type=pl.DeviceIdType.MESH
+        )
+
+    blocks = width // TILE
+    at = 0
+    for i in range(blocks):
+        for j in range(i, blocks):
+            part[at : at + TILE, :] = (
+                gram_ref[i * TILE : (i + 1) * TILE, j * TILE : (j + 1) * TILE] * scale
+            )
+            at += TILE
+    for j in range(blocks):
+        part[at : at + width, :] = term_ref[:, j * TILE : (j + 1) * TILE] * scale
+        at += width
+    pl.semaphore_wait(barrier, levels)
+
+    streams = range(len(orders))
+    offset = [[start] for start in starts]
+
+    def aligned(value):
+        return pl.multiple_of(value, 8)
+
+    def scatter(s, level):
+        size, halved = plans[s][level]
+        b = orders[s][level]
+        base = offset[s][-1]
+        if halved:
+            source = base + (1 - bit_of(b)) * size
+            offset[s].append(base + bit_of(b) * size)
+        else:
+            source = base
+            offset[s].append(base)
+        copy = pltpu.make_async_remote_copy(
+            src_ref=part.at[pl.ds(aligned(source), size)],
+            dst_ref=inbox.at[pl.ds(landing[s][level], size)],
+            send_sem=send_sem.at[s, level],
+            recv_sem=recv_sem.at[s, level],
+            device_id=device(b),
+            device_id_type=pl.DeviceIdType.MESH,
+        )
+        copy.start()
+        return copy
+
+    flying = [scatter(s, 0) for s in streams]
+    for level in range(levels):
+        for s in streams:
+            flying[s].wait()
+            size = plans[s][level][0]
+            here = pl.ds(aligned(offset[s][-1]), size)
+            total = part[here, :] + inbox[landing[s][level] : landing[s][level] + size, :]
+            if level + 1 < levels:
+                part[here, :] = total
+                flying[s] = scatter(s, level + 1)
+            else:
+                full[here, :] = total
+
+    def gather(s, level):
+        size, halved = plans[s][level]
+        if not halved:
+            return None
+        here = pl.ds(aligned(offset[s][level + 1]), size)
+        copy = pltpu.make_async_remote_copy(
+            src_ref=full.at[here],
+            dst_ref=full.at[here],
+            send_sem=send_sem.at[s, levels + level],
+            recv_sem=recv_sem.at[s, levels + level],
+            device_id=device(orders[s][level]),
+            device_id_type=pl.DeviceIdType.MESH,
+        )
+        copy.start()
+        return copy
+
+    flying = [gather(s, levels - 1) for s in streams]
+    for level in range(levels - 1, -1, -1):
+        for s in streams:
+            if flying[s] is not None:
+                flying[s].wait()
+            if level > 0:
+                flying[s] = gather(s, level - 1)
+
+    at = 0
+    for i in range(blocks):
+        for j in range(blocks):
+            here = (slice(i * TILE, (i + 1) * TILE), slice(j * TILE, (j + 1) * TILE))
+            if j < i:
+                gram_out[here] = jnp.zeros((TILE, TILE), jnp.float32)
+            else:
+                gram_out[here] = full[at : at + TILE, :]
+                at += TILE
+    for j in range(blocks):
+        term_out[:, j * TILE : (j + 1) * TILE] = full[at : at + width, :]
+        at += width
+
+
+def summed(gram, term, scale):
+    width = gram.shape[0]
+    levels = lax.axis_size(AXES).bit_length() - 1
+    blocks = width // TILE
+    packed = blocks * (blocks + 1) // 2 * TILE
+    half = blocks * width // 2
+    lengths = (packed, half, half)
+    starts = (0, packed, packed + half)
+    rest = list(range(1, levels))
+    orders = [[0] + rest[s:] + rest[:s] for s in range(3)]
+    plans = [level_plan(length, levels) for length in lengths]
+    landing = []
+    at = 0
+    for plan in plans:
+        places = []
+        for size, _ in plan:
+            places.append(at)
+            at += size
+        landing.append(places)
+    shape = jax.ShapeDtypeStruct((width, width), jnp.float32)
+    rows = sum(lengths)
+    return pl.pallas_call(
+        functools.partial(
+            sum_kernel, plans, orders, starts, landing, scale, width
+        ),
+        out_shape=(shape, shape),
+        in_specs=[pl.BlockSpec(memory_space=pltpu.VMEM)] * 2,
+        out_specs=(pl.BlockSpec(memory_space=pltpu.VMEM),) * 2,
+        scratch_shapes=[
+            pltpu.VMEM((rows, TILE), jnp.float32),
+            pltpu.VMEM((at, TILE), jnp.float32),
+            pltpu.VMEM((rows, TILE), jnp.float32),
+            pltpu.SemaphoreType.DMA((3, 2 * levels)),
+            pltpu.SemaphoreType.DMA((3, 2 * levels)),
+        ],
+        compiler_params=pltpu.CompilerParams(
+            collective_id=0,
+            has_side_effects=True,
+            vmem_limit_bytes=32 * 1024 * 1024,
+        ),
+        cost_estimate=pl.CostEstimate(
+            flops=rows * TILE, bytes_accessed=8 * rows * TILE, transcendentals=0
+        ),
+    )(gram, term)
+
+
 def from_behind(block):
     count = lax.axis_size(AXES)
     route = [(i - 1, i) for i in range(1, count)]
@@ -103,14 +279,13 @@
     local_gram = jnp.dot(
         snapshots.T, snapshots, precision=high, preferred_element_type=jnp.float32
     )
-    gram = lax.psum(local_gram, AXES) / count
     extended = jnp.concatenate([arrived, snapshots], 0)
     position = upstream - (first_row - EDGE)
     image = velocity[:, None] * (jnp.take(extended, position, axis=0) - snapshots)
     local_term = jnp.dot(
         snapshots.T, image, precision=high, preferred_element_type=jnp.float32
     )
-    term = lax.psum(local_term, AXES) / count
+    gram, term = summed(local_gram, local_term, 1.0 / count)
     upper, inverse = factor(gram)
     operator = dot32(dot32(inverse, term, ((1,), (0,))), inverse, ((1,), (1,)))
     return (operator, upper)

time: 220 us -> 109 us (0.50)
  waiting for transfers between devices: 143 us -> 0.01 us
  Pallas kernels: 26.3 us -> 76 us
  between operations: 14.1 us -> 0.71 us
  other arithmetic: 5.65 us -> 3.09 us
    psum x1 -> x0, waiting for transfers between devices: 143 us -> none  [shards(): gram = lax.psum(local_gram, AXES) / count]
    pallas_call x0 -> x1, Pallas kernels: none -> 49.7 us  [summed(): pl.pallas_call(functools.partial(sum_kernel, plans, orders, starts, landi...]
  transfers between devices with their start and end apart: 2 -> 1, of which waited for: 1 -> 0; matrix products, arithmetic and copies ran while one was open for 3% -> 6% of each run, Pallas kernels for 0% -> 0%
where the time goes in v1:
time: 109 us
  Pallas kernels  76 us (70%)
  matrix products  17.5 us (16%)
  local copies, waits for them, and re-layouts  9.22 us (8%)
  other arithmetic  3.09 us (3%)
  starting transfers between devices  2.42 us (2%)
    pallas_call x1, Pallas kernels, summed(): pl.pallas_call(functools.partial(sum_kernel, plans, orders, starts, landi...  49.7 us
    pallas_call x1, Pallas kernels, factor(): pl.pallas_call(factor_kernel, out_shape=(shape, shape), in_specs=[pl.Bloc...  26.3 us
    gather x1, local copies, waits for them, and re-layouts, shards(): jnp.take(extended, position, axis=0) - snapshots  7.92 us
    dot_general x1, matrix products, shards(): jnp.dot(snapshots.T, image, precision=high, preferred_element_type=jnp.fl...  7.16 us
    dot_general x1, matrix products, shards(): jnp.dot(snapshots.T, snapshots, precision=high, preferred_element_type=jn...  5.62 us
    dot_general x2, matrix products, dot32(): lax.dot_general(a, b, (dims, ((), ())), precision=lax.Precision.HIGHEST,...  4.68 us
    ppermute x1, starting transfers between devices, from_behind(): return lax.ppermute(block, AXES, route)  2.42 us
    concatenate x1, other arithmetic, shards(): extended = jnp.concatenate([arrived, snapshots], 0)  2.37 us
  transfers between devices with their start and end apart: 1, of which 0 were waited for; matrix products, arithmetic and copies ran while one was open for 6% of the time, Pallas kernels for 0%

profile of v1, /device:TPU:0, one launch (start us, length us, event | category | flops | bytes accessed | tf_op | source)
XLA Modules:
  0.0 108.9 jit_solution(13722361914165800242)
XLA Ops:
  0.6 1.3 %slice.3 = f32[512,512]{1,0:T(8,128)S(1)} slice(f32[1536,512]{1,0:T(8,128)} %param.3), slice={[1024:1536], [0:512]} | slice | bytes 2097152 | tf_op jit(solution)/shard_map/slice | solution.py:278
  1.9 2.4 %collective-permute-start = (f32[512,512]{1,0:T(8,128)S(1)}, f32[512,512]{1,0:T(8,128)S(1)}, u32[]{:S(2)}, u32[]{:S(2)}) collective-permute-start(f32[512,512]{1,0:T(8,128)S(1)} %slice.3), channel_id=1, source_target_pairs={{0,1},{1,2},{2,3},{3,4},{4,5},{5,6},{6,7},{7,8},{8,9},{9,10},{10,1... | collective-permute-start | bytes 3145736 | tf_op jit(solution)/shard_map/ppermute | solution.py:270
  4.4 0.7 compare_and_fusion
  5.1 0.0 copy-start
  5.1 5.6 %fusion.11.gram_ref = f32[512,512]{1,0:T(8,128)S(1)} fusion(f32[1536,512]{1,0:T(8,128)} %param.3), kind=kOutput, calls=%fused_computation.14 | convolution fusion | flops 2415919104 | bytes 4194304 | tf_op jit(solution)/shard_map/dot_general | solution.py:279
  10.7 0.0 collective-permute-done
  10.7 0.0 copy-done
  10.7 2.4 %pad_maximum_fusion = f32[2048,512]{1,0:T(8,128)} fusion(f32[1536,512]{1,0:T(8,128)S(1)} %copy-done, f32[512,512]{1,0:T(8,128)S(1)} %collective-permute-done), kind=kLoop, calls=%fused_computation.1 | loop fusion | flops 1048576 | bytes 8388608 | tf_op jit(solution)/shard_map/concatenate | solution.py:282
  13.1 0.0 copy-start.1
  13.1 7.9 %gather_fusion = f32[1536,512]{1,0:T(8,128)} fusion(f32[2048,512]{1,0:T(8,128)} %pad_maximum_fusion, s32[2048]{0:T(1024)S(1)} %pad_clamp_fusion), kind=kCustom, calls=%fused_computation | custom fusion | bytes 6297600 | tf_op jit(solution)/shard_map/jit(_take)/gather | solution.py:284
  21.0 0.0 copy-done.1
  21.0 7.2 %fusion.7.term_ref = f32[512,512]{1,0:T(8,128)S(1)} fusion(f32[1536,512]{1,0:T(8,128)} %param.3, f32[1536,512]{1,0:T(8,128)} %gather_fusion, f32[1536]{0:T(1024)S(1)} %copy-done.1, pred[1536]{0:T(1024)(128)(4,1)S(1)} %get-tuple-element.10), kind=kOutput, calls=%fused_computation.9 | convolution fusion | flops 2418278400 | bytes 7347712 | tf_op jit(solution)/shard_map/dot_general | solution.py:285
  28.2 49.7 %shard_map.50 = (f32[512,512]{1,0:T(8,128)S(1)}, f32[512,512]{1,0:T(8,128)S(1)}) custom-call(f32[512,512]{1,0:T(8,128)S(1)} %fusion.11.gram_ref, f32[512,512]{1,0:T(8,128)S(1)} %fusion.7.term_ref), custom_call_target="tpu_custom_call" | custom-call | flops 425984 | bytes 3407872 | tf_op jit(solution)/shard_map/pallas_call | solution.py:242
  77.9 26.3 %shard_map.51 = (f32[512,512]{1,0:T(8,128)}, f32[512,512]{1,0:T(8,128)S(1)}) custom-call(f32[512,512]{1,0:T(8,128)S(1)} %get-tuple-element.6.gram_ref), custom_call_target="tpu_custom_call" | custom-call | flops 1610612736 | bytes 3145728 | tf_op jit(solution)/shard_map/pallas_call | solution.py:80
  104.2 1.8 %fusion.12 = f32[512,512]{1,0:T(8,128)S(1)} fusion(f32[512,512]{1,0:T(8,128)S(1)} %get-tuple-element.7, f32[512,512]{1,0:T(8,128)S(1)} %get-tuple-element.8), kind=kOutput, calls=%fused_computation.15 | convolution fusion | flops 1610612736 | bytes 3145728 | tf_op jit(solution)/shard_map/dot_general | solution.py:17
  106.0 2.8 %fusion.13 = f32[512,512]{1,0:T(8,128)} fusion(f32[512,512]{1,0:T(8,128)S(1)} %fusion.12, f32[512,512]{1,0:T(8,128)S(1)} %get-tuple-element.7), kind=kOutput, calls=%fused_computation.16 | convolution fusion | flops 1610612736 | bytes 3145728 | tf_op jit(solution)/shard_map/dot_general | solution.py:17
  (1 shorter events, 0.0 us)
Async XLA Ops:
  1.9 8.8 %collective-permute-start = (f32[512,512]{1,0:T(8,128)S(1)}, f32[512,512]{1,0:T(8,128)S(1)}, u32[]{:S(2)}, u32[]{:S(2)}) collective-permute-start(f32[512,512]{1,0:T(8,128)S(1)} %slice.3), channel_id=1, source_target_pairs={{0,1},{1,2},{2,3},{3,4},{4,5},{5,6},{6,7},{7,8},{8,9},{9,10},{10,1... | collective-permute-start | bytes 3145736 | tf_op jit(solution)/shard_map/ppermute | solution.py:270
  5.1 5.7 %copy-start = (f32[1536,512]{1,0:T(8,128)S(1)}, f32[1536,512]{1,0:T(8,128)}, u32[]{:S(2)}) copy-start(f32[1536,512]{1,0:T(8,128)} %param.3) | copy-start | bytes 9437188
  13.1 7.9 %copy-start.1 = (f32[1536]{0:T(1024)S(1)}, f32[1536]{0:T(1024)}, u32[]{:S(2)}) copy-start(f32[1536]{0:T(1024)} %param.5) | copy-start | bytes 18436

commit v2 on v1

--- a/solution.py
+++ b/solution.py
@@ -105,14 +105,30 @@
     return sizes
 
 
+def halves(value):
+    top = value.astype(jnp.bfloat16)
+    return top, (value - top.astype(jnp.float32)).astype(jnp.bfloat16)
+
+
+def product(a, b, dims):
+    return lax.dot_general(a, b, (dims, ((), ())), preferred_element_type=jnp.float32)
+
+
+def column(ref, lo, hi, lanes):
+    spread = jnp.broadcast_to(ref[:, lo:hi], (TILE, hi - lo)).T
+    return jnp.concatenate([spread] * (lanes // TILE), 1)
+
+
 def sum_kernel(
     plans, orders, starts, landing, scale, width,
-    gram_ref, term_ref, gram_out, term_out,
-    part, inbox, full, send_sem, recv_sem,
+    snap_ref, up_ref, vel_ref, gram_out, term_out,
+    top, low, halo, part, inbox, full, send_sem, recv_sem, halo_sem,
 ):
     minor = lax.axis_size("grp")
+    devices = lax.axis_size("seg") * minor
     me = lax.axis_index("seg") * minor + lax.axis_index("grp")
     levels = len(orders[0])
+    rows = snap_ref.shape[0]
 
     def bit_of(b):
         return (me // (1 << b)) % 2
@@ -121,88 +137,134 @@
         other = me + (1 - 2 * bit_of(b)) * (1 << b)
         return (other // minor, other % minor)
 
+    ahead = (me + 1) % devices
+    behind = (me + devices - 1) % devices
     barrier = pltpu.get_barrier_semaphore()
     for b in range(levels):
         pl.semaphore_signal(
             barrier, inc=1, device_id=device(b), device_id_type=pl.DeviceIdType.MESH
         )
-
+    pl.semaphore_signal(
+        barrier,
+        inc=1,
+        device_id=(behind // minor, behind % minor),
+        device_id_type=pl.DeviceIdType.MESH,
+    )
+    for lo in range(0, rows, EDGE):
+        t, l = halves(snap_ref[lo : lo + EDGE, :])
+        top[lo : lo + EDGE, :] = t
+        low[lo : lo + EDGE, :] = l
+    both = ((0,), (0,))
+    lead = product(top[...], top[...], both)
+    cross = product(top[...], low[...], both)
     blocks = width // TILE
     at = 0
     for i in range(blocks):
         for j in range(i, blocks):
+            si, sj = slice(i * TILE, (i + 1) * TILE), slice(j * TILE, (j + 1) * TILE)
             part[at : at + TILE, :] = (
-                gram_ref[i * TILE : (i + 1) * TILE, j * TILE : (j + 1) * TILE] * scale
-            )
+                lead[si, sj] + (cross[si, sj] + cross[sj, si].T)
+            ) * scale
             at += TILE
-    for j in range(blocks):
-        part[at : at + width, :] = term_ref[:, j * TILE : (j + 1) * TILE] * scale
-        at += width
-    pl.semaphore_wait(barrier, levels)
-
-    streams = range(len(orders))
-    offset = [[start] for start in starts]
+    pl.semaphore_wait(barrier, levels + 1)
 
     def aligned(value):
         return pl.multiple_of(value, 8)
 
-    def scatter(s, level):
-        size, halved = plans[s][level]
-        b = orders[s][level]
-        base = offset[s][-1]
-        if halved:
-            source = base + (1 - bit_of(b)) * size
-            offset[s].append(base + bit_of(b) * size)
-        else:
-            source = base
-            offset[s].append(base)
-        copy = pltpu.make_async_remote_copy(
-            src_ref=part.at[pl.ds(aligned(source), size)],
-            dst_ref=inbox.at[pl.ds(landing[s][level], size)],
-            send_sem=send_sem.at[s, level],
-            recv_sem=recv_sem.at[s, level],
-            device_id=device(b),
-            device_id_type=pl.DeviceIdType.MESH,
-        )
-        copy.start()
-        return copy
-
-    flying = [scatter(s, 0) for s in streams]
-    for level in range(levels):
-        for s in streams:
-            flying[s].wait()
-            size = plans[s][level][0]
-            here = pl.ds(aligned(offset[s][-1]), size)
-            total = part[here, :] + inbox[landing[s][level] : landing[s][level] + size, :]
+    def stream(s):
+        offset = [starts[s]]
+        for level in range(levels):
+            size, halved = plans[s][level]
+            b = orders[s][level]
+            base = offset[-1]
+            source = base + (1 - bit_of(b)) * size if halved else base
+            kept = base + bit_of(b) * size if halved else base
+            offset.append(kept)
+            land = landing[s][level]
+            copy = pltpu.make_async_remote_copy(
+                src_ref=part.at[pl.ds(aligned(source), size)],
+                dst_ref=inbox.at[pl.ds(land, size)],
+                send_sem=send_sem.at[s, level],
+                recv_sem=recv_sem.at[s, level],
+                device_id=device(b),
+                device_id_type=pl.DeviceIdType.MESH,
+            )
+            copy.start()
+            yield
+            copy.wait()
+            here = pl.ds(aligned(kept), size)
+            total = part[here, :] + inbox[land : land + size, :]
             if level + 1 < levels:
                 part[here, :] = total
-                flying[s] = scatter(s, level + 1)
             else:
                 full[here, :] = total
-
-    def gather(s, level):
-        size, halved = plans[s][level]
-        if not halved:
-            return None
-        here = pl.ds(aligned(offset[s][level + 1]), size)
-        copy = pltpu.make_async_remote_copy(
-            src_ref=full.at[here],
-            dst_ref=full.at[here],
-            send_sem=send_sem.at[s, levels + level],
-            recv_sem=recv_sem.at[s, levels + level],
-            device_id=device(orders[s][level]),
-            device_id_type=pl.DeviceIdType.MESH,
+        for level in range(levels - 1, -1, -1):
+            size, halved = plans[s][level]
+            if halved:
+                here = pl.ds(aligned(offset[level + 1]), size)
+                copy = pltpu.make_async_remote_copy(
+                    src_ref=full.at[here],
+                    dst_ref=full.at[here],
+                    send_sem=send_sem.at[s, levels + level],
+                    recv_sem=recv_sem.at[s, levels + level],
+                    device_id=device(orders[s][level]),
+                    device_id_type=pl.DeviceIdType.MESH,
+                )
+                copy.start()
+                yield
+                copy.wait()
+
+    def advance(running):
+        return [g for g in running if next(g, True) is None]
+
+    halo_copy = pltpu.make_async_remote_copy(
+        src_ref=snap_ref.at[pl.ds(rows - EDGE, EDGE)],
+        dst_ref=halo,
+        send_sem=halo_sem.at[0],
+        recv_sem=halo_sem.at[1],
+        device_id=(ahead // minor, ahead % minor),
+        device_id_type=pl.DeviceIdType.MESH,
+    )
+    running = advance([stream(s) for s in range(3)])
+    halo_copy.start()
+    first_row = me * rows
+
+    def share(lo, source_top, source_low, origin):
+        hi = lo + EDGE
+        span = source_top.shape[0]
+        wanted = column(up_ref, lo, hi, TILE) - origin
+        lane = lax.broadcasted_iota(jnp.int32, (EDGE, TILE), 1)
+        pick = jnp.concatenate(
+            [
+                jnp.where(wanted == lane + c, 1.0, 0.0).astype(jnp.bfloat16)
+                for c in range(0, span, TILE)
+            ],
+            1,
         )
-        copy.start()
-        return copy
-
-    flying = [gather(s, levels - 1) for s in streams]
-    for level in range(levels - 1, -1, -1):
-        for s in streams:
-            if flying[s] is not None:
-                flying[s].wait()
-            if level > 0:
-                flying[s] = gather(s, level - 1)
+        along = ((1,), (0,))
+        feed = product(pick, source_top, along) + product(pick, source_low, along)
+        image = column(vel_ref, lo, hi, width) * (feed - snap_ref[lo:hi, :])
+        it, il = halves(image)
+        return product(top[lo:hi, :], it, both) + (
+            product(top[lo:hi, :], il, both) + product(low[lo:hi, :], it, both)
+        )
+
+    term = None
+    for lo in range(EDGE, rows, EDGE):
+        more = share(lo, top[: lo + EDGE, :], low[: lo + EDGE, :], first_row)
+        term = more if term is None else term + more
+        running = advance(running)
+    halo_copy.wait()
+    arrived = jnp.where(me > 0, halo[...], 0.0)
+    ht, hl = halves(arrived)
+    term = term + share(0, ht, hl, first_row - EDGE)
+    at = starts[3]
+    for j in range(blocks):
+        part[at : at + width, :] = term[:, j * TILE : (j + 1) * TILE] * scale
+        at += width
+    running = running + advance([stream(s) for s in range(3, len(orders))])
+    while running:
+        running = advance(running)
 
     at = 0
     for i in range(blocks):
@@ -218,16 +280,23 @@
         at += width
 
 
-def summed(gram, term, scale):
-    width = gram.shape[0]
+def thirds(rows):
+    unit = 256 if rows % 256 == 0 else 8
+    units = rows // unit
+    first = -(-units // 3)
+    second = -(-(units - first) // 2)
+    return [first * unit, second * unit, (units - first - second) * unit]
+
+
+def summed(snapshots, upstream, velocity, scale):
+    rows_here, width = snapshots.shape
     levels = lax.axis_size(AXES).bit_length() - 1
     blocks = width // TILE
     packed = blocks * (blocks + 1) // 2 * TILE
-    half = blocks * width // 2
-    lengths = (packed, half, half)
-    starts = (0, packed, packed + half)
+    lengths = thirds(packed) + thirds(blocks * width)
+    starts = [sum(lengths[:s]) for s in range(len(lengths))]
     rest = list(range(1, levels))
-    orders = [[0] + rest[s:] + rest[:s] for s in range(3)]
+    orders = [[0] + rest[s:] + rest[:s] for s in (0, 1, 2)] * 2
     plans = [level_plan(length, levels) for length in lengths]
     landing = []
     at = 0
@@ -240,52 +309,37 @@
     shape = jax.ShapeDtypeStruct((width, width), jnp.float32)
     rows = sum(lengths)
     return pl.pallas_call(
-        functools.partial(
-            sum_kernel, plans, orders, starts, landing, scale, width
-        ),
+        functools.partial(sum_kernel, plans, orders, starts, landing, scale, width),
         out_shape=(shape, shape),
-        in_specs=[pl.BlockSpec(memory_space=pltpu.VMEM)] * 2,
+        in_specs=[pl.BlockSpec(memory_space=pltpu.VMEM)] * 3,
         out_specs=(pl.BlockSpec(memory_space=pltpu.VMEM),) * 2,
         scratch_shapes=[
+            pltpu.VMEM((rows_here, width), jnp.bfloat16),
+            pltpu.VMEM((rows_here, width), jnp.bfloat16),
+            pltpu.VMEM((EDGE, width), jnp.float32),
             pltpu.VMEM((rows, TILE), jnp.float32),
             pltpu.VMEM((at, TILE), jnp.float32),
             pltpu.VMEM((rows, TILE), jnp.float32),
-            pltpu.SemaphoreType.DMA((3, 2 * levels)),
-            pltpu.SemaphoreType.DMA((3, 2 * levels)),
+            pltpu.SemaphoreType.DMA((len(lengths), 2 * levels)),
+            pltpu.SemaphoreType.DMA((len(lengths), 2 * levels)),
+            pltpu.SemaphoreType.DMA((2,)),
         ],
         compiler_params=pltpu.CompilerParams(
             collective_id=0,
             has_side_effects=True,
-            vmem_limit_bytes=32 * 1024 * 1024,
+            vmem_limit_bytes=48 * 1024 * 1024,
         ),
         cost_estimate=pl.CostEstimate(
-            flops=rows * TILE, bytes_accessed=8 * rows * TILE, transcendentals=0
+            flops=24 * rows_here * width**2,
+            bytes_accessed=8 * rows * TILE,
+            transcendentals=0,
         ),
-    )(gram, term)
-
-
-def from_behind(block):
-    count = lax.axis_size(AXES)
-    route = [(i - 1, i) for i in range(1, count)]
-    return lax.ppermute(block, AXES, route)
+    )(snapshots, upstream[None, :], velocity[None, :])
 
 
 def shards(snapshots, upstream, velocity):
-    high = lax.Precision.HIGH
-    rows_here = snapshots.shape[0]
-    count = rows_here * lax.axis_size(AXES)
-    first_row = lax.axis_index(AXES) * rows_here
-    arrived = from_behind(snapshots[rows_here - EDGE :])
-    local_gram = jnp.dot(
-        snapshots.T, snapshots, precision=high, preferred_element_type=jnp.float32
-    )
-    extended = jnp.concatenate([arrived, snapshots], 0)
-    position = upstream - (first_row - EDGE)
-    image = velocity[:, None] * (jnp.take(extended, position, axis=0) - snapshots)
-    local_term = jnp.dot(
-        snapshots.T, image, precision=high, preferred_element_type=jnp.float32
-    )
-    gram, term = summed(local_gram, local_term, 1.0 / count)
+    count = snapshots.shape[0] * lax.axis_size(AXES)
+    gram, term = summed(snapshots, upstream, velocity, 1.0 / count)
     upper, inverse = factor(gram)
     operator = dot32(dot32(inverse, term, ((1,), (0,))), inverse, ((1,), (1,)))
     return (operator, upper)

time: 109 us -> 89.6 us (0.82)
  matrix products: 17.5 us -> 4.68 us
  local copies, waits for them, and re-layouts: 9.22 us -> 3.29 us
  Pallas kernels: 76 us -> 80.7 us
  other arithmetic: 3.09 us -> 0 us
  starting transfers between devices: 2.42 us -> 0 us
    dot_general x2 -> x0, matrix products: 12.8 us -> none  [the longest x1 7.16 us: shards(): jnp.dot(snapshots.T, image, precision=high, preferred_element_type=jnp.fl...]
    gather x1 -> x0, local copies, waits for them, and re-layouts: 7.92 us -> none  [shards(): jnp.take(extended, position, axis=0) - snapshots]
    pallas_call x1, Pallas kernels: 49.7 us -> 54.4 us  [summed(): pl.pallas_call(functools.partial(sum_kernel, plans, orders, starts, landi...]
    ppermute x1 -> x0, starting transfers between devices: 2.42 us -> none  [from_behind(): return lax.ppermute(block, AXES, route)]
    concatenate x1 -> x0, other arithmetic: 2.37 us -> none  [shards(): extended = jnp.concatenate([arrived, snapshots], 0)]
    unnamed x4 -> x2, local copies, waits for them, and re-layouts: 0.01 us -> 1.89 us
    broadcast_in_dim x0 -> x2, local copies, waits for them, and re-layouts: none -> 1.4 us  [the longest x1 0.7 us: summed(): upstream[None, :]]
    slice x1 -> x0, local copies, waits for them, and re-layouts: 1.3 us -> none  [shards(): arrived = from_behind(snapshots[rows_here - EDGE:])]
  transfers between devices with their start and end apart: 1 -> 0, of which waited for: 0 -> 0; matrix products, arithmetic and copies ran while one was open for 6% -> 0% of each run, Pallas kernels for 0% -> 0%
where the time goes in v2:
time: 89.6 us; the launch traced here: 89.3 us
  Pallas kernels  80.7 us (90%)
  matrix products  4.68 us (5%)
  local copies, waits for them, and re-layouts  3.29 us (4%)
    pallas_call x1, Pallas kernels, summed(): pl.pallas_call(functools.partial(sum_kernel, plans, orders, starts, landi...  54.4 us
    pallas_call x1, Pallas kernels, factor(): pl.pallas_call(factor_kernel, out_shape=(shape, shape), in_specs=[pl.Bloc...  26.3 us
    dot_general x2, matrix products, dot32(): lax.dot_general(a, b, (dims, ((), ())), precision=lax.Precision.HIGHEST,...  4.68 us
    unnamed x2, local copies, waits for them, and re-layouts  1.89 us

profile of v2, /device:TPU:0, one launch (start us, length us, event | category | flops | bytes accessed | tf_op | source)
XLA Modules:
  0.0 89.3 jit_solution(7035039056621276397)
XLA Ops:
  0.6 0.7 broadcast_in_dim.6.up_ref
  1.3 0.7 broadcast_in_dim.7.vel_ref
  2.0 0.0 copy-start
  2.0 1.9 %copy-done = f32[1536,512]{1,0:T(8,128)S(1)} copy-done((f32[1536,512]{1,0:T(8,128)S(1)}, f32[1536,512]{1,0:T(8,128)}, u32[]{:S(2)}) %copy-start) | copy-done | bytes 3145752
  3.9 54.4 %shard_map.50 = (f32[512,512]{1,0:T(8,128)S(1)}, f32[512,512]{1,0:T(8,128)S(1)}) custom-call(f32[1536,512]{1,0:T(8,128)S(1)} %copy-done, s32[1,1536]{1,0:T(1,128)S(1)} %broadcast_in_dim.6.up_ref, f32[1,1536]{1,0:T(1,128)S(1)} %broadcast_in_dim.7.vel_ref), custom_call_target="tpu_custom_call" | custom-call | flops 9663676416 | bytes 3407872 | tf_op jit(solution)/shard_map/pallas_call | solution.py:311
  58.4 26.3 %shard_map.51 = (f32[512,512]{1,0:T(8,128)}, f32[512,512]{1,0:T(8,128)S(1)}) custom-call(f32[512,512]{1,0:T(8,128)S(1)} %get-tuple-element.6.gram_ref), custom_call_target="tpu_custom_call" | custom-call | flops 1610612736 | bytes 3145728 | tf_op jit(solution)/shard_map/pallas_call | solution.py:80
  84.6 1.8 %fusion = f32[512,512]{1,0:T(8,128)S(1)} fusion(f32[512,512]{1,0:T(8,128)S(1)} %get-tuple-element.7, f32[512,512]{1,0:T(8,128)S(1)} %get-tuple-element.8), kind=kOutput, calls=%fused_computation | convolution fusion | flops 1610612736 | bytes 3145728 | tf_op jit(solution)/shard_map/dot_general | solution.py:17
  86.5 2.8 %fusion.1 = f32[512,512]{1,0:T(8,128)} fusion(f32[512,512]{1,0:T(8,128)S(1)} %fusion, f32[512,512]{1,0:T(8,128)S(1)} %get-tuple-element.7), kind=kOutput, calls=%fused_computation.1 | convolution fusion | flops 1610612736 | bytes 3145728 | tf_op jit(solution)/shard_map/dot_general | solution.py:17
Async XLA Ops:
  2.0 1.9 %copy-start = (f32[1536,512]{1,0:T(8,128)S(1)}, f32[1536,512]{1,0:T(8,128)}, u32[]{:S(2)}) copy-start(f32[1536,512]{1,0:T(8,128)} %snap_ref.1) | copy-start | bytes 9437188

commit v3 on v2

--- a/solution.py
+++ b/solution.py
@@ -53,9 +53,8 @@
     return jnp.where(keep, work, 0.0)
 
 
-def factor_kernel(gram_ref, upper_ref, inverse_ref, a_ref):
-    order = gram_ref.shape[0]
-    a_ref[...] = gram_ref[...]
+def factor(a_ref, upper_ref, inverse_ref, between):
+    order = a_ref.shape[0]
     upper_ref[...] = jnp.zeros_like(upper_ref)
     r = lax.broadcasted_iota(jnp.int32, (order, order), 0)
     c = lax.broadcasted_iota(jnp.int32, (order, order), 1)
@@ -63,31 +62,21 @@
     for lo in range(0, order, NB):
         hi = lo + NB
         done = eliminate(a_ref[lo:hi, lo:hi])
+        between()
         inv = done[:, NB:]
+        reach = -(-hi // TILE) * TILE
+        new = dot32(inv, inverse_ref[lo:hi, :reach], ((1,), (0,)))
+        if hi < order:
+            start = hi // TILE * TILE
+            line = dot32(inv, a_ref[lo:hi, start:], ((1,), (0,)))
+            a_ref[start:, start:] = a_ref[start:, start:] - dot32(line, line, ((0,), (0,)))
+            inverse_ref[start:, :reach] = inverse_ref[start:, :reach] - dot32(
+                line, new, ((0,), (0,))
+            )
+            upper_ref[lo:hi, start:] = line
         upper_ref[lo:hi, lo:hi] = done[:, :NB]
-        new = dot32(inv, inverse_ref[lo:hi, :], ((1,), (0,)))
-        inverse_ref[lo:hi, :] = new
-        if hi < order:
-            line = dot32(inv, a_ref[lo:hi, hi:], ((1,), (0,)))
-            upper_ref[lo:hi, hi:] = line
-            a_ref[hi:, hi:] = a_ref[hi:, hi:] - dot32(line, line, ((0,), (0,)))
-            inverse_ref[hi:, :] = inverse_ref[hi:, :] - dot32(line, new, ((0,), (0,)))
-
-
-def factor(gram):
-    order = gram.shape[0]
-    shape = jax.ShapeDtypeStruct((order, order), jnp.float32)
-    return pl.pallas_call(
-        factor_kernel,
-        out_shape=(shape, shape),
-        in_specs=[pl.BlockSpec(memory_space=pltpu.VMEM)],
-        out_specs=(pl.BlockSpec(memory_space=pltpu.VMEM),) * 2,
-        scratch_shapes=[pltpu.VMEM((order, order), jnp.float32)],
-        compiler_params=pltpu.CompilerParams(vmem_limit_bytes=32 * 1024 * 1024),
-        cost_estimate=pl.CostEstimate(
-            flops=12 * order**3, bytes_accessed=12 * order**2, transcendentals=0
-        ),
-    )(gram)
+        inverse_ref[lo:hi, :reach] = new
+        between()
 
 
 TILE = 128
@@ -121,8 +110,8 @@
 
 def sum_kernel(
     plans, orders, starts, landing, scale, width,
-    snap_ref, up_ref, vel_ref, gram_out, term_out,
-    top, low, halo, part, inbox, full, send_sem, recv_sem, halo_sem,
+    snap_ref, up_ref, vel_ref, operator_out, upper_out,
+    gram, inverse, top, low, halo, part, inbox, full, send_sem, recv_sem, halo_sem,
 ):
     minor = lax.axis_size("grp")
     devices = lax.axis_size("seg") * minor
@@ -262,7 +251,7 @@
     for j in range(blocks):
         part[at : at + width, :] = term[:, j * TILE : (j + 1) * TILE] * scale
         at += width
-    running = running + advance([stream(s) for s in range(3, len(orders))])
+    later = advance([stream(s) for s in range(3, len(orders))])
     while running:
         running = advance(running)
 
@@ -271,13 +260,25 @@
         for j in range(blocks):
             here = (slice(i * TILE, (i + 1) * TILE), slice(j * TILE, (j + 1) * TILE))
             if j < i:
-                gram_out[here] = jnp.zeros((TILE, TILE), jnp.float32)
+                gram[here] = jnp.zeros((TILE, TILE), jnp.float32)
             else:
-                gram_out[here] = full[at : at + TILE, :]
+                gram[here] = full[at : at + TILE, :]
                 at += TILE
+
+    pending = [later]
+
+    def between():
+        pending[0] = advance(pending[0])
+
+    factor(gram, upper_out, inverse, between)
+    while pending[0]:
+        between()
     for j in range(blocks):
-        term_out[:, j * TILE : (j + 1) * TILE] = full[at : at + width, :]
+        gram[:, j * TILE : (j + 1) * TILE] = full[at : at + width, :]
         at += width
+    along = ((1,), (0,))
+    left = dot32(inverse[...], gram[...], along)
+    operator_out[...] = dot32(left, inverse[...], ((1,), (1,)))
 
 
 def thirds(rows):
@@ -288,7 +289,7 @@
     return [first * unit, second * unit, (units - first - second) * unit]
 
 
-def summed(snapshots, upstream, velocity, scale):
+def projected(snapshots, upstream, velocity, scale):
     rows_here, width = snapshots.shape
     levels = lax.axis_size(AXES).bit_length() - 1
     blocks = width // TILE
@@ -314,6 +315,8 @@
         in_specs=[pl.BlockSpec(memory_space=pltpu.VMEM)] * 3,
         out_specs=(pl.BlockSpec(memory_space=pltpu.VMEM),) * 2,
         scratch_shapes=[
+            pltpu.VMEM((width, width), jnp.float32),
+            pltpu.VMEM((width, width), jnp.float32),
             pltpu.VMEM((rows_here, width), jnp.bfloat16),
             pltpu.VMEM((rows_here, width), jnp.bfloat16),
             pltpu.VMEM((EDGE, width), jnp.float32),
@@ -339,10 +342,7 @@
 
 def shards(snapshots, upstream, velocity):
     count = snapshots.shape[0] * lax.axis_size(AXES)
-    gram, term = summed(snapshots, upstream, velocity, 1.0 / count)
-    upper, inverse = factor(gram)
-    operator = dot32(dot32(inverse, term, ((1,), (0,))), inverse, ((1,), (1,)))
-    return (operator, upper)
+    return projected(snapshots, upstream, velocity, 1.0 / count)
 
 
 def solution(mesh):

time: 89.6 us -> 98.9 us (1.10)
  Pallas kernels: 80.7 us -> 92.8 us
  matrix products: 4.68 us -> 0 us
  local copies, waits for them, and re-layouts: 3.29 us -> 5.23 us
    pallas_call x2 -> x1, Pallas kernels: 80.7 us -> 92.8 us  [projected(): pl.pallas_call(functools.partial(sum_kernel, plans, orders, starts, landi...]
    dot_general x2 -> x0, matrix products: 4.68 us -> none  [dot32(): lax.dot_general(a, b, (dims, ((), ())), precision=lax.Precision.HIGHEST,...]
    unnamed x2 -> x4, local copies, waits for them, and re-layouts: 1.89 us -> 3.83 us
where the time goes in v3:
time: 98.9 us; the launch traced here: 98.7 us
  Pallas kernels  92.8 us (94%)
  local copies, waits for them, and re-layouts  5.23 us (5%)
    pallas_call x1, Pallas kernels, projected(): pl.pallas_call(functools.partial(sum_kernel, plans, orders, starts, landi...  92.8 us
    unnamed x4, local copies, waits for them, and re-layouts  3.83 us

profile of v3, /device:TPU:0, one launch (start us, length us, event | category | flops | bytes accessed | tf_op | source)
XLA Modules:
  0.0 98.7 jit_solution(12129145029822686339)
XLA Ops:
  0.6 0.7 broadcast_in_dim.6.up_ref
  1.3 0.7 broadcast_in_dim.7.vel_ref
  2.0 0.0 copy-start
  2.0 1.9 %copy-done = f32[1536,512]{1,0:T(8,128)S(1)} copy-done((f32[1536,512]{1,0:T(8,128)S(1)}, f32[1536,512]{1,0:T(8,128)}, u32[]{:S(2)}) %copy-start) | copy-done | bytes 3145752
  3.9 92.8 %shard_map.50 = (f32[512,512]{1,0:T(8,128)S(1)}, f32[512,512]{1,0:T(8,128)S(1)}) custom-call(f32[1536,512]{1,0:T(8,128)S(1)} %copy-done, s32[1,1536]{1,0:T(1,128)S(1)} %broadcast_in_dim.6.up_ref, f32[1,1536]{1,0:T(1,128)S(1)} %broadcast_in_dim.7.vel_ref), custom_call_target="tpu_custom_call" | custom-call | flops 9663676416 | bytes 3407872 | tf_op jit(solution)/shard_map/pallas_call | solution.py:312
  96.7 1.0 copy.7
  97.7 1.0 copy.8
Async XLA Ops:
  2.0 1.9 %copy-start = (f32[1536,512]{1,0:T(8,128)S(1)}, f32[1536,512]{1,0:T(8,128)}, u32[]{:S(2)}) copy-start(f32[1536,512]{1,0:T(8,128)} %snap_ref.1) | copy-start | bytes 9437188

commit v4 on v2

--- a/solution.py
+++ b/solution.py
@@ -10,6 +10,7 @@
 EDGE = 512
 NB = 64
 GROUP = 4
+TILE = 128
 AXES = ("seg", "grp")
 
 
@@ -64,14 +65,18 @@
         hi = lo + NB
         done = eliminate(a_ref[lo:hi, lo:hi])
         inv = done[:, NB:]
+        reach = -(-hi // TILE) * TILE
+        new = dot32(inv, inverse_ref[lo:hi, :reach], ((1,), (0,)))
+        if hi < order:
+            start = hi // TILE * TILE
+            line = dot32(inv, a_ref[lo:hi, start:], ((1,), (0,)))
+            a_ref[start:, start:] = a_ref[start:, start:] - dot32(line, line, ((0,), (0,)))
+            inverse_ref[start:, :reach] = inverse_ref[start:, :reach] - dot32(
+                line, new, ((0,), (0,))
+            )
+            upper_ref[lo:hi, start:] = line
         upper_ref[lo:hi, lo:hi] = done[:, :NB]
-        new = dot32(inv, inverse_ref[lo:hi, :], ((1,), (0,)))
-        inverse_ref[lo:hi, :] = new
-        if hi < order:
-            line = dot32(inv, a_ref[lo:hi, hi:], ((1,), (0,)))
-            upper_ref[lo:hi, hi:] = line
-            a_ref[hi:, hi:] = a_ref[hi:, hi:] - dot32(line, line, ((0,), (0,)))
-            inverse_ref[hi:, :] = inverse_ref[hi:, :] - dot32(line, new, ((0,), (0,)))
+        inverse_ref[lo:hi, :reach] = new
 
 
 def factor(gram):
@@ -88,9 +93,6 @@
             flops=12 * order**3, bytes_accessed=12 * order**2, transcendentals=0
         ),
     )(gram)
-
-
-TILE = 128
 
 
 def level_plan(rows, levels):

time: 89.6 us -> 88.5 us (0.988)
  Pallas kernels: 80.7 us -> 79.6 us
    pallas_call x1, Pallas kernels: 26.3 us -> 25.2 us  [factor(): pl.pallas_call(factor_kernel, out_shape=(shape, shape), in_specs=[pl.Bloc...]
where the time goes in v4:
time: 88.5 us; the launch traced here: 88.2 us
  Pallas kernels  79.6 us (90%)
  matrix products  4.68 us (5%)
  local copies, waits for them, and re-layouts  3.29 us (4%)
    pallas_call x1, Pallas kernels, summed(): pl.pallas_call(functools.partial(sum_kernel, plans, orders, starts, landi...  54.4 us
    pallas_call x1, Pallas kernels, factor(): pl.pallas_call(factor_kernel, out_shape=(shape, shape), in_specs=[pl.Bloc...  25.2 us
    dot_general x2, matrix products, dot32(): lax.dot_general(a, b, (dims, ((), ())), precision=lax.Precision.HIGHEST,...  4.68 us
    unnamed x2, local copies, waits for them, and re-layouts  1.89 us

profile of v4, /device:TPU:0, one launch (start us, length us, event | category | flops | bytes accessed | tf_op | source)
XLA Modules:
  0.0 88.2 jit_solution(1258539397813659771)
XLA Ops:
  0.6 0.7 broadcast_in_dim.6.up_ref
  1.3 0.7 broadcast_in_dim.7.vel_ref
  2.0 0.0 copy-start
  2.0 1.9 %copy-done = f32[1536,512]{1,0:T(8,128)S(1)} copy-done((f32[1536,512]{1,0:T(8,128)S(1)}, f32[1536,512]{1,0:T(8,128)}, u32[]{:S(2)}) %copy-start) | copy-done | bytes 3145752
  3.9 54.4 %shard_map.50 = (f32[512,512]{1,0:T(8,128)S(1)}, f32[512,512]{1,0:T(8,128)S(1)}) custom-call(f32[1536,512]{1,0:T(8,128)S(1)} %copy-done, s32[1,1536]{1,0:T(1,128)S(1)} %broadcast_in_dim.6.up_ref, f32[1,1536]{1,0:T(1,128)S(1)} %broadcast_in_dim.7.vel_ref), custom_call_target="tpu_custom_call" | custom-call | flops 9663676416 | bytes 3407872 | tf_op jit(solution)/shard_map/pallas_call | solution.py:313
  58.4 25.2 %shard_map.51 = (f32[512,512]{1,0:T(8,128)}, f32[512,512]{1,0:T(8,128)S(1)}) custom-call(f32[512,512]{1,0:T(8,128)S(1)} %get-tuple-element.6.gram_ref), custom_call_target="tpu_custom_call" | custom-call | flops 1610612736 | bytes 3145728 | tf_op jit(solution)/shard_map/pallas_call | solution.py:85
  83.5 1.8 %fusion = f32[512,512]{1,0:T(8,128)S(1)} fusion(f32[512,512]{1,0:T(8,128)S(1)} %get-tuple-element.7, f32[512,512]{1,0:T(8,128)S(1)} %get-tuple-element.8), kind=kOutput, calls=%fused_computation | convolution fusion | flops 1610612736 | bytes 3145728 | tf_op jit(solution)/shard_map/dot_general | solution.py:18
  85.4 2.8 %fusion.1 = f32[512,512]{1,0:T(8,128)} fusion(f32[512,512]{1,0:T(8,128)S(1)} %fusion, f32[512,512]{1,0:T(8,128)S(1)} %get-tuple-element.7), kind=kOutput, calls=%fused_computation.1 | convolution fusion | flops 1610612736 | bytes 3145728 | tf_op jit(solution)/shard_map/dot_general | solution.py:18
Async XLA Ops:
  2.0 1.9 %copy-start = (f32[1536,512]{1,0:T(8,128)S(1)}, f32[1536,512]{1,0:T(8,128)}, u32[]{:S(2)}) copy-start(f32[1536,512]{1,0:T(8,128)} %snap_ref.1) | copy-start | bytes 9437188
